TPU v7x, 32 devices: a whole 2x2x4 slice. The times are simulated.
32 devices in a mesh: groups: 2 (over y), expert: 16 (over z, x, core), head: 1.
Axes of the slice: x: 2, y: 2, z: 4, core: 2. Of those that a mesh axis runs over, the one named last changes fastest.
Arguments:
- sources: bfloat16 [4096, 1024], P(('groups', 'expert')), parts along dimension 0, may hold values from -6 to 6
- enc_gain: float32 [1024], replicated, may hold values from 0.1 to 1.9
- route_ids: int32 [4096, 2], P(('groups', 'expert')), parts along dimension 0, may hold values from 0 to 7, all different within a row; in each aligned block of 128 rows (0 to 127, 128 to 255, ...) at most 40 rows name the same one
- route_gates: float32 [4096, 2], P(('groups', 'expert')), parts along dimension 0, may hold values from 0.2 to 1
- w_in: bfloat16 [16, 1024, 2048], P('expert', None, 'head'), may hold values from -0.1875 to 0.1875
- w_out: bfloat16 [16, 2048, 1024], P('expert', 'head'), may hold values from -0.09375 to 0.09375
- targets: bfloat16 [4096, 1024], P(('groups', 'expert')), parts along dimension 0, may hold values from -6 to 6
- dec_gain: float32 [1024], replicated, may hold values from 0.1 to 1.9
- src_lengths: int32 [64], P(('groups', 'expert')), parts along dimension 0, may hold values from 16 to 64, as said below
- tgt_lengths: int32 [64], P(('groups', 'expert')), parts along dimension 0, may hold values from 16 to 64, as said below
- w_query: bfloat16 [1024, 1024], P('expert', 'head'), may hold values from -60 to 60
- w_key: bfloat16 [1024, 1024], P('expert', 'head'), may hold values from -0.1875 to 0.1875
- w_value: bfloat16 [1024, 1024], P('expert', 'head'), may hold values from -0.1875 to 0.1875
- w_attn: bfloat16 [1024, 1024], P('expert', 'head'), may hold values from -0.1875 to 0.1875
Outputs:
- memory: bfloat16 [4096, 1024], P(('groups', 'expert')), parts along dimension 0
- decoded: bfloat16 [4096, 1024], P(('groups', 'expert'), 'head'), parts along dimension 0
There are 2 independent parts, one for each index of `groups`. A program takes and returns all parts, laid end to end along the dimension named above; an argument that names none is the same for every part. Nothing has to cross between parts.
Inputs may be any that keep to these rules, and one draw needn't show every extreme that they name: `route_ids`: in each aligned block of 128 rows no expert is named more than 40 times, a bound that some block reaches. `src_lengths`: some sentence has exactly 64 live tokens. `tgt_lengths`: some sentence has exactly 64 live tokens.
All inputs are finite; a program needn't handle non-finite values.
Results may differ from a plain program's by a relative error of at most 0.025.
Values may be sent and summed in bfloat16 or wider, within the bound.
No kernel may reach another device: no remote copies, remote signals or barrier semaphores. Data moves between devices by JAX's collectives and lax.ppermute only.
A program may use at most 64 MiB of HBM per device.

v0:
```python
import jax
import jax.numpy as jnp
from jax import lax
from jax.sharding import PartitionSpec as P

DH = 64


def from_partner(x, axis, stride):
    return lax.ppermute(x, axis, [(i, i ^ 1 << stride) for i in range(lax.axis_size(axis))])


def layer_norm(rows, gain):
    rows = rows.astype(jnp.float32)
    mean = jnp.mean(rows, axis=-1, keepdims=True)
    centered = rows - mean
    spread = jnp.mean(centered * centered, axis=-1, keepdims=True)
    return centered * lax.rsqrt(spread + 1e-05) * gain


def partner(block):
    return from_partner(block, "expert", 0)


def shards(
    sources,
    enc_gain,
    route_ids,
    route_gates,
    w_in,
    w_out,
    targets,
    dec_gain,
    src_lengths,
    tgt_lengths,
    w_query,
    w_key,
    w_value,
    w_attn,
):
    tok_rows, width = sources.shape
    experts = lax.axis_size("expert") // 2
    capacity = 2 * ((5 * tok_rows + 4 * experts - 1) // (4 * experts))
    side = lax.axis_index("expert") % 2
    pair_ids = route_ids.reshape(-1)
    onehot = (pair_ids[:, None] == jnp.arange(experts, dtype=jnp.int32)[None, :]).astype(jnp.int32)
    earlier = jnp.cumsum(onehot, axis=0) - onehot
    slots = jnp.sum(earlier * onehot, axis=1)
    place = pair_ids * capacity + slots
    normed = layer_norm(sources, enc_gain).astype(jnp.bfloat16)
    outgoing = (
        jnp.zeros((experts * capacity, width), jnp.bfloat16)
        .at[place]
        .set(jnp.repeat(normed, 2, axis=0))
    )
    sending = outgoing.reshape(2 * experts, capacity // 2, width)
    arrived = lax.all_to_all(sending, "expert", split_axis=0, concat_axis=0, tiled=True)
    other = partner(arrived)
    lower = jnp.where(side == 0, arrived, other)
    upper = jnp.where(side == 0, other, arrived)
    arrived = jnp.concatenate((lower, upper), axis=1)
    expert_rows = arrived.reshape(-1, width)
    hidden = jnp.maximum(
        jnp.dot(expert_rows, w_in[0], preferred_element_type=jnp.float32), 0.0
    ).astype(jnp.bfloat16)
    quarter = jnp.dot(hidden, w_out[0], preferred_element_type=jnp.float32)
    half = lax.psum(quarter.astype(jnp.bfloat16), "head")
    kept = half.shape[1]
    half = half.reshape(2 * experts, capacity, kept)
    other_half = partner(half)
    merged = (half.astype(jnp.float32) + other_half.astype(jnp.float32)).astype(jnp.bfloat16)
    leaving = lax.dynamic_slice_in_dim(merged, side * (capacity // 2), capacity // 2, 1)
    returned = lax.all_to_all(leaving, "expert", split_axis=0, concat_axis=0, tiled=True)
    results = returned.reshape(-1, kept)
    picked = jnp.take(results, place, axis=0).astype(jnp.float32).reshape(tok_rows, 2, kept)
    moe = route_gates[:, 0:1] * picked[:, 0, :] + route_gates[:, 1:2] * picked[:, 1, :]
    memory = (sources.astype(jnp.float32) + moe).astype(jnp.bfloat16)
    w_q, w_k, w_v, w_o = (
        lax.all_gather(w_query, "expert", axis=0, tiled=True),
        lax.all_gather(w_key, "expert", axis=0, tiled=True),
        lax.all_gather(w_value, "expert", axis=0, tiled=True),
        lax.all_gather(w_attn, "expert", axis=0, tiled=True),
    )
    tnormed = layer_norm(targets, dec_gain).astype(jnp.bfloat16)
    query = jnp.dot(tnormed, w_q, preferred_element_type=jnp.float32).astype(jnp.bfloat16)
    key = jnp.dot(memory, w_k, preferred_element_type=jnp.float32).astype(jnp.bfloat16)
    value = jnp.dot(memory, w_v, preferred_element_type=jnp.float32).astype(jnp.bfloat16)
    sentences = src_lengths.shape[0]
    local_heads = query.shape[1] // DH
    queries = query.reshape(sentences, -1, local_heads, DH)
    keys = key.reshape(sentences, -1, local_heads, DH)
    values = value.reshape(sentences, -1, local_heads, DH)
    key_count = keys.shape[1]
    scores = jnp.einsum(
        "sqhd,skhd->shqk", queries, keys, preferred_element_type=jnp.float32
    ) * DH ** (-0.5)
    live = jnp.arange(key_count, dtype=jnp.int32)[None, :] < src_lengths[:, None]
    scores = jnp.where(live[:, None, None, :], scores, -1e30)
    top = jnp.max(scores, axis=-1, keepdims=True)
    raised = jnp.exp(scores - top)
    weights = (raised / jnp.sum(raised, axis=-1, keepdims=True)).astype(jnp.bfloat16)
    context = jnp.einsum(
        "shqk,skhd->sqhd", weights, values, preferred_element_type=jnp.float32
    ).astype(jnp.bfloat16)
    context = context.reshape(targets.shape[0], -1)
    partial_out = lax.dot_general(
        context, w_o, (((1,), (1,)), ((), ())), preferred_element_type=jnp.float32
    )
    attn = lax.psum_scatter(
        partial_out.astype(jnp.bfloat16), "head", scatter_dimension=1, tiled=True
    ).astype(jnp.float32)
    share = width // lax.axis_size("head")
    own_targets = lax.dynamic_slice_in_dim(
        targets, lax.axis_index("head") * share, share, 1
    ).astype(jnp.float32)
    per_sentence = targets.shape[0] // sentences
    positions = jnp.arange(targets.shape[0], dtype=jnp.int32)
    owner = positions // per_sentence
    live_rows = (positions % per_sentence < jnp.take(tgt_lengths, owner)).astype(jnp.float32)
    decoded = ((own_targets + attn) * live_rows[:, None]).astype(jnp.bfloat16)
    return (memory, decoded)


def solution(mesh):
    placed = (
        P(("groups", "expert"), None),
        P(),
        P(("groups", "expert"), None),
        P(("groups", "expert"), None),
        P("expert", None, "head"),
        P("expert", "head", None),
        P(("groups", "expert"), None),
        P(),
        P(("groups", "expert")),
        P(("groups", "expert")),
        P("expert", "head"),
        P("expert", "head"),
        P("expert", "head"),
        P("expert", "head"),
    )
    return jax.shard_map(
        shards,
        mesh=mesh,
        in_specs=placed,
        out_specs=(P(("groups", "expert"), None), P(("groups", "expert"), "head")),
        check_vma=False,
    )
```

profile of v0, /device:TPU:0, one launch (start us, length us, event | category | flops | bytes accessed | tf_op | source)
XLA Modules:
  0.0 201.6 jit_solution(6229918482698029241)
XLA Ops:
  7.2 0.7 all-gather.7.cloned.1.call-update
  7.9 0.7 all-gather.5.cloned.1.call-update
  8.6 0.8 copy.44
  9.7 0.7 broadcast_multiply_fusion
  10.7 0.6 reduce-window.6
  11.5 1.1 convert_reduce_fusion.1
  12.6 1.2 fusion.27
  13.8 1.2 fusion.29
  15.5 1.9 scatter_custom_fusion
  17.4 1.0 reshape.206
  18.5 7.4 %all-to-all-start = ((bf16[16,20,1024]{2,1,0:T(8,128)(2,1)}), bf16[16,20,1024]{2,1,0:T(8,128)(2,1)S(1)}, u32[]{:S(2)}, u32[]{:S(2)}) async-start(bf16[16,20,1024]{2,1,0:T(8,128)(2,1)} %reshape.206), calls=%async_computation | async-start | bytes 1572864 | tf_op jit(solution)/shard_map/all_to_all | solution.py:57
  25.9 0.7 all-gather.9.cloned.1.call-update
  26.6 19.0 %all-to-all-done = bf16[16,20,1024]{2,1,0:T(8,128)(2,1)S(1)} async-done(((bf16[16,20,1024]{2,1,0:T(8,128)(2,1)}), bf16[16,20,1024]{2,1,0:T(8,128)(2,1)S(1)}, u32[]{:S(2)}, u32[]{:S(2)}) %all-to-all-start) | async-done | bytes 655392 | tf_op jit(solution)/shard_map/all_to_all | solution.py:57
  46.3 1.9 collective-permute-done
  48.9 9.1 %fusion.7 = bf16[640,1024]{1,0:T(8,128)(2,1)S(1)} fusion(bf16[1,2048,1024]{2,1,0:T(8,128)(2,1)} %param.19, bf16[640,1024]{1,0:T(8,128)(2,1)S(1)} %bitcast.61, bf16[1,1024,2048]{2,1,0:T(8,128)(2,1)} %param.18), kind=kOutput, calls=%fused_computation.8 | convolution fusion | flops 5371985920 | bytes 11010048 | tf_op jit(solution)/shard_map/dot_general | solution.py:66
  58.4 0.6 fusion.55
  59.4 1.8 collective-permute-done.1
  61.1 1.5 add_convert_fusion
  62.6 11.7 %all-to-all-start.1 = ((bf16[16,20,1024]{2,1,0:T(8,128)(2,1)}), bf16[16,20,1024]{2,1,0:T(8,128)(2,1)S(1)}, u32[]{:S(2)}, u32[]{:S(2)}) async-start(bf16[16,20,1024]{2,1,0:T(8,128)(2,1)} %add_convert_fusion), calls=%async_computation.1 | async-start | bytes 1572864 | tf_op jit(solution)/shard_map/all_to_all | solution.py:73
  74.3 1.3 compare_convert_fusion
  76.0 2.1 %convolution_convert_fusion.3 = bf16[128,1024]{1,0:T(8,128)(2,1)S(1)} fusion(bf16[1024,1024]{1,0:T(8,128)(2,1)} %all-gather.7.cloned.1.call-done, bf16[128,1024]{1,0:T(8,128)(2,1)S(1)} %copy-done, f32[1024]{0:T(1024)S(1)} %copy-done.4, f32[128]{0:T(128)S(1)} %add_rsqrt_fusion, f32[128]{0:T(128)S(1)} %broadcast_multiply_fusion.1), kind=kOutput, calls=%fused_computation.23 | convolution fusion | flops 269221888 | bytes 2626560 | tf_op jit(solution)/shard_map/dot_general | solution.py:85
  78.5 15.5 %all-to-all-done.1 = bf16[16,20,1024]{2,1,0:T(8,128)(2,1)S(1)} async-done(((bf16[16,20,1024]{2,1,0:T(8,128)(2,1)}), bf16[16,20,1024]{2,1,0:T(8,128)(2,1)S(1)}, u32[]{:S(2)}, u32[]{:S(2)}) %all-to-all-start.1) | async-done | bytes 655392 | tf_op jit(solution)/shard_map/all_to_all | solution.py:73
  94.1 1.2 gather_fusion
  96.4 10.8 %all-gather.5.cloned.1.call-done = bf16[1024,1024]{1,0:T(8,128)(2,1)} async-done(((bf16[64,1024]{1,0:T(8,128)(2,1)}), bf16[1024,1024]{1,0:T(8,128)(2,1)}) %all-gather.5.cloned.1.call-update) | async-done | bytes 2097168 | tf_op jit(solution)/shard_map/all_gather | solution.py:81
  107.3 2.0 %convolution_convert_fusion.4 = bf16[128,1024]{1,0:T(8,128)(2,1)S(1)} fusion(bf16[128,1024]{1,0:T(8,128)(2,1)S(1)} %fusion.30, bf16[1024,1024]{1,0:T(8,128)(2,1)} %all-gather.5.cloned.1.call-done), kind=kOutput, calls=%fused_computation.24 | convolution fusion | flops 268566528 | bytes 2621440 | tf_op jit(solution)/shard_map/dot_general | solution.py:87
  109.7 40.1 %all-gather.9.cloned.1.call-done = bf16[1024,1024]{1,0:T(8,128)(2,1)} async-done(((bf16[64,1024]{1,0:T(8,128)(2,1)}), bf16[1024,1024]{1,0:T(8,128)(2,1)}) %all-gather.9.cloned.1.call-update) | async-done | bytes 2097168 | tf_op jit(solution)/shard_map/all_gather | solution.py:80
  149.8 2.0 %convolution_convert_fusion.2 = bf16[128,1024]{1,0:T(8,128)(2,1)S(1)} fusion(bf16[128,1024]{1,0:T(8,128)(2,1)S(1)} %fusion.30, bf16[1024,1024]{1,0:T(8,128)(2,1)} %all-gather.9.cloned.1.call-done), kind=kOutput, calls=%fused_computation.22 | convolution fusion | flops 268566528 | bytes 2621440 | tf_op jit(solution)/shard_map/dot_general | solution.py:86
  152.2 0.6 fusion.56
  152.7 1.4 fusion.12
  154.1 2.0 %fusion.13 = bf16[2,64,16,64]{1,3,2,0:T(8,128)(2,1)S(1)} fusion(bf16[2,64,16,64]{3,2,1,0:T(8,128)(2,1)S(1)} %reshape.210, f32[2,16,64]{2,1,0:T(8,128)S(1)} %fusion.56, f32[2,16,64,64]{2,3,1,0:T(8,128)} %fusion.12), kind=kOutput, calls=%fused_computation.16 | convolution fusion | flops 17303616 | bytes 1056768 | tf_op jit(solution)/shard_map/shqk,skhd->sqhd/dot_general | solution.py:102
  157.0 35.0 %all-gather.11.cloned.1.call-done = bf16[1024,1024]{1,0:T(8,128)(2,1)} async-done(((bf16[64,1024]{1,0:T(8,128)(2,1)}), bf16[1024,1024]{1,0:T(8,128)(2,1)}) %all-gather.11.cloned.1.call-update) | async-done | bytes 2097168 | tf_op jit(solution)/shard_map/all_gather | solution.py:82
  192.0 3.1 %fusion.17 = bf16[128,1024]{1,0:T(8,128)(2,1)} fusion(bf16[128,1024]{1,0:T(8,128)(2,1)S(1)} %reshape.213, bf16[1024,1024]{1,0:T(8,128)(2,1)} %all-gather.11.cloned.1.call-done, bf16[128,1024]{1,0:T(8,128)(2,1)S(1)} %copy-done, f32[128]{0:T(128)S(1)} %compare_convert_fusion), kind=kOutput, calls=%fused_computation.21 | convolution fusion | flops 269221888 | bytes 2884096 | tf_op jit(solution)/shard_map/dot_general | solution.py:106
  (60 shorter events, 6.9 us)
Async XLA Ops:
  7.2 68.9 %all-gather.7.cloned.1.call-start = ((), (), s32[]{:S(2)}) async-start(), calls=%async_computation.3 | async-start | bytes 2228224 | tf_op jit(solution)/shard_map/all_gather | solution.py:79
  7.9 99.4 %all-gather.5.cloned.1.call-start = ((), (), s32[]{:S(2)}) async-start(), calls=%async_computation.2 | async-start | bytes 2228224 | tf_op jit(solution)/shard_map/all_gather | solution.py:81
  18.5 27.2 %all-to-all-start = ((bf16[16,20,1024]{2,1,0:T(8,128)(2,1)}), bf16[16,20,1024]{2,1,0:T(8,128)(2,1)S(1)}, u32[]{:S(2)}, u32[]{:S(2)}) async-start(bf16[16,20,1024]{2,1,0:T(8,128)(2,1)} %reshape.206), calls=%async_computation | async-start | bytes 1572864 | tf_op jit(solution)/shard_map/all_to_all | solution.py:57
  25.8 123.9 %all-gather.9.cloned.1.call-start = ((), (), s32[]{:S(2)}) async-start(), calls=%async_computation.4 | async-start | bytes 2228224 | tf_op jit(solution)/shard_map/all_gather | solution.py:80
  26.6 165.4 %all-gather.11.cloned.1.call-start = ((), (), s32[]{:S(2)}) async-start(), calls=%async_computation.5 | async-start | bytes 2228224 | tf_op jit(solution)/shard_map/all_gather | solution.py:82
  46.0 2.2 %collective-permute-start = (bf16[16,20,1024]{2,0,1:T(8,128)(2,1)S(1)}, bf16[16,20,1024]{2,0,1:T(8,128)(2,1)S(1)}, u32[]{:S(2)}, u32[]{:S(2)}) collective-permute-start(bf16[16,20,1024]{2,0,1:T(8,128)(2,1)S(1)} %copy.48), channel_id=1, source_target_pairs={{0,1},{1,0},{2,3},{3,2},{4,5},{5,4},{6,7},{7,6},{8,9},{9,8},{10,11... | collective-permute-start | bytes 1966088 | tf_op jit(solution)/shard_map/ppermute | solution.py:10
  48.9 9.5 %copy-start.5 = (s32[2]{0:T(128)S(1)}, s32[2]{0:T(128)}, u32[]{:S(2)}) copy-start(s32[2]{0:T(128)} %param.23) | copy-start | bytes 28
  48.9 10.1 %copy-start = (bf16[128,1024]{1,0:T(8,128)(2,1)S(1)}, bf16[128,1024]{1,0:T(8,128)(2,1)}, u32[]{:S(2)}) copy-start(bf16[128,1024]{1,0:T(8,128)(2,1)} %param.20) | copy-start | bytes 786436
  58.0 3.1 %collective-permute-start.1 = (bf16[16,40,1024]{2,1,0:T(8,128)(2,1)S(1)}, bf16[16,40,1024]{2,1,0:T(8,128)(2,1)S(1)}, u32[]{:S(2)}, u32[]{:S(2)}) collective-permute-start(bf16[16,40,1024]{2,1,0:T(8,128)(2,1)S(1)} %bitcast.62), channel_id=1, source_target_pairs={{0,1},{1,0},{2,3},{3,2},{4,5},{5,4},{6,7},{7,6},{8,9},{9,8},{10,11... | collective-permute-start | bytes 3932168 | tf_op jit(solution)/shard_map/ppermute | solution.py:10
  59.3 16.6 %copy-start.7 = (s32[2]{0:T(128)S(1)}, s32[2]{0:T(128)}, u32[]{:S(2)}) copy-start(s32[2]{0:T(128)} %param.22) | copy-start | bytes 28
  59.3 16.6 %copy-start.6 = (f32[128,2]{0,1:T(2,128)S(1)}, f32[128,2]{0,1:T(2,128)}, u32[]{:S(2)}) copy-start(f32[128,2]{0,1:T(2,128)} %param.17) | copy-start | bytes 3076
  59.3 16.6 %copy-start.3 = (s32[128,2]{0,1:T(2,128)S(1)}, s32[128,2]{0,1:T(2,128)}, u32[]{:S(2)}) copy-start(s32[128,2]{0,1:T(2,128)} %param.16) | copy-start | bytes 3076
  59.3 16.7 %copy-start.4 = (f32[1024]{0:T(1024)S(1)}, f32[1024]{0:T(1024)}, u32[]{:S(2)}) copy-start(f32[1024]{0:T(1024)} %param.21) | copy-start | bytes 12292
  62.6 31.4 %all-to-all-start.1 = ((bf16[16,20,1024]{2,1,0:T(8,128)(2,1)}), bf16[16,20,1024]{2,1,0:T(8,128)(2,1)S(1)}, u32[]{:S(2)}, u32[]{:S(2)}) async-start(bf16[16,20,1024]{2,1,0:T(8,128)(2,1)} %add_convert_fusion), calls=%async_computation.1 | async-start | bytes 1572864 | tf_op jit(solution)/shard_map/all_to_all | solution.py:73
  95.3 1.0 copy-start.1
  96.4 55.4 %copy-start.2 = (bf16[128,1024]{1,0:T(8,128)(2,1)}, bf16[128,1024]{1,0:T(8,128)(2,1)S(1)}, u32[]{:S(2)}) copy-start(bf16[128,1024]{1,0:T(8,128)(2,1)S(1)} %fusion.30) | copy-start | bytes 786436
Sparse Core Ops, SparseCore 0:
  10.2 49.3 all-gather.6
  61.7 45.5 all-gather.4
  109.4 40.2 all-gather.8
  151.8 40.1 all-gather.10
where the time goes:
time: 202 us
  waiting for transfers between devices  126 us (62%)
  matrix products  22.4 us (11%)
  starting transfers between devices  19.8 us (10%)
  between operations  14.1 us (7%)
  local copies, waits for them, and re-layouts  9.9 us (5%)
  other arithmetic  9.17 us (5%)
    all_gather x1, waiting for transfers between devices, shards(): lax.all_gather(w_key, 'expert', axis=0, tiled=True)  40.1 us
    all_gather x1, waiting for transfers between devices, shards(): lax.all_gather(w_attn, 'expert', axis=0, tiled=True)  35 us
    all_to_all x1, waiting for transfers between devices, shards(): lax.all_to_all(sending, 'expert', split_axis=0, concat_axis=0, tiled=True)  19 us
    all_to_all x1, waiting for transfers between devices, shards(): lax.all_to_all(leaving, 'expert', split_axis=0, concat_axis=0, tiled=True)  15.5 us
    all_to_all x1, starting transfers between devices, shards(): lax.all_to_all(leaving, 'expert', split_axis=0, concat_axis=0, tiled=True)  11.7 us
    all_gather x1, waiting for transfers between devices, shards(): lax.all_gather(w_value, 'expert', axis=0, tiled=True)  10.8 us
    dot_general x1, matrix products, shards(): quarter = jnp.dot(hidden, w_out[0], preferred_element_type=jnp.float32)  9.11 us
    all_to_all x1, starting transfers between devices, shards(): lax.all_to_all(sending, 'expert', split_axis=0, concat_axis=0, tiled=True)  7.36 us
  transfers between devices with their start and end apart: 8, of which 7 were waited for; matrix products, arithmetic and copies ran while one was open for 19% of the time, Pallas kernels for 0%

commit v1 on v0

--- a/solution.py
+++ b/solution.py
@@ -4,6 +4,33 @@
 from jax.sharding import PartitionSpec as P
 
 DH = 64
+
+
+def step_on_the_object(x_local, dim_k):
+    left_arr = list(x_local.shape[1:])
+    left_arr[dim_k] *= x_local.shape[0]
+    even = jnp.moveaxis(x_local, 0, dim_k).reshape(left_arr)
+    return even
+
+
+def _detail_axis_part(slab_in, bus_axis):
+    block_last, fresh = (lax.axis_size(bus_axis), lax.axis_index(bus_axis))
+    part_next, f_now = (slab_in[None], 1)
+    while f_now < block_last:
+        reached = lax.ppermute(
+            part_next, bus_axis, perm=list(map(lambda rr: (rr, rr ^ f_now), range(block_last)))
+        )
+        built = fresh & f_now == 0
+        part_next = jnp.concatenate(
+            [jnp.where(built, part_next, reached), jnp.where(built, reached, part_next)]
+        )
+        f_now *= 2
+    return part_next
+
+
+def cover_works_now(content, my_tile, axis_k):
+    step_out = step_on_the_object(_detail_axis_part(content, my_tile), axis_k)
+    return step_out
 
 
 def from_partner(x, axis, stride):
@@ -79,7 +106,7 @@
         lax.all_gather(w_query, "expert", axis=0, tiled=True),
         lax.all_gather(w_key, "expert", axis=0, tiled=True),
         lax.all_gather(w_value, "expert", axis=0, tiled=True),
-        lax.all_gather(w_attn, "expert", axis=0, tiled=True),
+        cover_works_now(w_attn, "expert", 0),
     )
     tnormed = layer_norm(targets, dec_gain).astype(jnp.bfloat16)
     query = jnp.dot(tnormed, w_q, preferred_element_type=jnp.float32).astype(jnp.bfloat16)

time: 202 us -> 191 us (0.946)
  waiting for transfers between devices: 126 us -> 93 us
  starting transfers between devices: 19.8 us -> 28.8 us
  other arithmetic: 9.17 us -> 15.4 us
  local copies, waits for them, and re-layouts: 9.9 us -> 14.4 us
  matrix products: 22.4 us -> 24.9 us
    ppermute x0 -> x4, waiting for transfers between devices: none -> 62.8 us  [_detail_axis_part(): lax.ppermute(part_next, bus_axis, perm=list(map(lambda rr: (rr, rr ^ f_no...]
    all_gather x1, waiting for transfers between devices: 40.1 us -> 0.02 us  [shards(): lax.all_gather(w_key, 'expert', axis=0, tiled=True)]
    all_gather x1 -> x0, waiting for transfers between devices: 35 us -> none  [shards(): lax.all_gather(w_attn, 'expert', axis=0, tiled=True)]
    ppermute x0 -> x4, starting transfers between devices: none -> 16.2 us  [_detail_axis_part(): lax.ppermute(part_next, bus_axis, perm=list(map(lambda rr: (rr, rr ^ f_no...]
    all_to_all x1, waiting for transfers between devices: 15.5 us -> 3.67 us  [shards(): lax.all_to_all(leaving, 'expert', split_axis=0, concat_axis=0, tiled=True)]
    all_to_all x1, starting transfers between devices: 11.7 us -> 4.46 us  [shards(): lax.all_to_all(leaving, 'expert', split_axis=0, concat_axis=0, tiled=True)]
    all_gather x1, waiting for transfers between devices: 10.8 us -> 6.87 us  [shards(): lax.all_gather(w_value, 'expert', axis=0, tiled=True)]
    ppermute x2, waiting for transfers between devices: 3.64 us -> 0.01 us  [from_partner(): lax.ppermute(x, axis, [(i, i ^ 1 << stride) for i in range(lax.axis_size(...]
  transfers between devices with their start and end apart: 8 -> 11, of which waited for: 7 -> 7; matrix products, arithmetic and copies ran while one was open for 19% -> 24% of each run, Pallas kernels for 0% -> 0%
where the time goes in v1:
time: 191 us
  waiting for transfers between devices  93 us (49%)
  starting transfers between devices  28.8 us (15%)
  matrix products  24.9 us (13%)
  other arithmetic  15.4 us (8%)
  local copies, waits for them, and re-layouts  14.4 us (8%)
  between operations  14.1 us (7%)
    ppermute x4, waiting for transfers between devices, _detail_axis_part(): lax.ppermute(part_next, bus_axis, perm=list(map(lambda rr: (rr, rr ^ f_no...  62.8 us
    all_to_all x1, waiting for transfers between devices, shards(): lax.all_to_all(sending, 'expert', split_axis=0, concat_axis=0, tiled=True)  18.1 us
    ppermute x4, starting transfers between devices, _detail_axis_part(): lax.ppermute(part_next, bus_axis, perm=list(map(lambda rr: (rr, rr ^ f_no...  16.2 us
    dot_general x1, matrix products, shards(): quarter = jnp.dot(hidden, w_out[0], preferred_element_type=jnp.float32)  10.1 us
    all_to_all x1, starting transfers between devices, shards(): lax.all_to_all(sending, 'expert', split_axis=0, concat_axis=0, tiled=True)  7.49 us
    all_gather x1, waiting for transfers between devices, shards(): lax.all_gather(w_value, 'expert', axis=0, tiled=True)  6.87 us
    all_to_all x1, starting transfers between devices, shards(): lax.all_to_all(leaving, 'expert', split_axis=0, concat_axis=0, tiled=True)  4.46 us
  transfers between devices with their start and end apart: 11, of which 7 were waited for; matrix products, arithmetic and copies ran while one was open for 24% of the time, Pallas kernels for 0%

profile of v1, /device:TPU:0, one launch (start us, length us, event | category | flops | bytes accessed | tf_op | source)
XLA Modules:
  0.0 190.6 jit_solution(14941596026519301896)
XLA Ops:
  11.5 1.1 convert_reduce_fusion.1
  12.6 1.2 fusion.27
  13.8 1.2 fusion.29
  15.6 1.9 scatter_custom_fusion
  18.4 7.5 %all-to-all-start = ((bf16[16,20,1024]{2,1,0:T(8,128)(2,1)}), bf16[16,20,1024]{2,1,0:T(8,128)(2,1)S(1)}, u32[]{:S(2)}, u32[]{:S(2)}) async-start(bf16[16,20,1024]{2,1,0:T(8,128)(2,1)} %reshape.209), calls=%async_computation | async-start | bytes 1572864 | tf_op jit(solution)/shard_map/all_to_all | solution.py:84
  27.5 18.1 %all-to-all-done = bf16[16,20,1024]{2,1,0:T(8,128)(2,1)S(1)} async-done(((bf16[16,20,1024]{2,1,0:T(8,128)(2,1)}), bf16[16,20,1024]{2,1,0:T(8,128)(2,1)S(1)}, u32[]{:S(2)}, u32[]{:S(2)}) %all-to-all-start) | async-done | bytes 655392 | tf_op jit(solution)/shard_map/all_to_all | solution.py:84
  46.5 4.3 %collective-permute-start.3 = (bf16[2,64,1024]{2,1,0:T(8,128)(2,1)S(1)}, bf16[2,64,1024]{2,1,0:T(8,128)(2,1)S(1)}, u32[]{:S(2)}, u32[]{:S(2)}) collective-permute-start(bf16[2,64,1024]{2,1,0:T(8,128)(2,1)S(1)} %pad_maximum_fusion.4), channel_id=1, source_target_pairs={{0,2},{1,3},{2,0},{3,1},{4,6},{5,7},{6,4},{7,5},{8,10},{9,11},{10,... | collective-permute-start | bytes 786440 | tf_op jit(solution)/shard_map/ppermute | solution.py:20
  50.9 6.3 %collective-permute-done.3 = bf16[2,64,1024]{2,1,0:T(8,128)(2,1)S(1)} collective-permute-done((bf16[2,64,1024]{2,1,0:T(8,128)(2,1)S(1)}, bf16[2,64,1024]{2,1,0:T(8,128)(2,1)S(1)}, u32[]{:S(2)}, u32[]{:S(2)}) %collective-permute-start.3) | collective-permute-done | bytes 262176 | tf_op jit(solution)/shard_map/ppermute | solution.py:20
  58.2 5.6 %collective-permute-start.4 = (bf16[4,64,1024]{2,1,0:T(8,128)(2,1)}, bf16[4,64,1024]{2,1,0:T(8,128)(2,1)}, u32[]{:S(2)}, u32[]{:S(2)}) collective-permute-start(bf16[4,64,1024]{2,1,0:T(8,128)(2,1)} %pad_maximum_fusion.3), channel_id=1, source_target_pairs={{0,4},{1,5},{2,6},{3,7},{4,0},{5,1},{6,2},{7,3},{8,12},{9,13},{10,... | collective-permute-start | bytes 1572872 | tf_op jit(solution)/shard_map/ppermute | solution.py:20
  64.4 10.1 %fusion.7 = bf16[640,1024]{1,0:T(8,128)(2,1)} fusion(bf16[1,2048,1024]{2,1,0:T(8,128)(2,1)} %param.19, bf16[640,1024]{1,0:T(8,128)(2,1)S(1)} %bitcast.66, bf16[1,1024,2048]{2,1,0:T(8,128)(2,1)} %param.18), kind=kOutput, calls=%fused_computation.9 | convolution fusion | flops 5371985920 | bytes 11010048 | tf_op jit(solution)/shard_map/dot_general | solution.py:93
  74.8 3.5 %collective-permute-done.4 = bf16[4,64,1024]{2,1,0:T(8,128)(2,1)} collective-permute-done((bf16[4,64,1024]{2,1,0:T(8,128)(2,1)}, bf16[4,64,1024]{2,1,0:T(8,128)(2,1)}, u32[]{:S(2)}, u32[]{:S(2)}) %collective-permute-start.4) | collective-permute-done | bytes 524320 | tf_op jit(solution)/shard_map/ppermute | solution.py:20
  78.4 1.1 broadcast_select_fusion.5
  79.6 6.0 %collective-permute-start.5 = (bf16[8,64,1024]{2,1,0:T(8,128)(2,1)S(1)}, bf16[8,64,1024]{2,1,0:T(8,128)(2,1)S(1)}, u32[]{:S(2)}, u32[]{:S(2)}) collective-permute-start(bf16[8,64,1024]{2,1,0:T(8,128)(2,1)S(1)} %pad_maximum_fusion.2), channel_id=1, source_target_pairs={{0,8},{1,9},{2,10},{3,11},{4,12},{5,13},{6,14},{7,15},{8,0},{9,1},... | collective-permute-start | bytes 3145736 | tf_op jit(solution)/shard_map/ppermute | solution.py:20
  86.8 3.0 %add_convert_fusion = bf16[16,20,1024]{2,1,0:T(8,128)(2,1)} fusion(bf16[16,40,1024]{2,1,0:T(8,128)(2,1)} %collective-permute-done.1, s32[]{:T(128)S(6)} %select_n.159, bf16[16,40,1024]{2,1,0:T(8,128)(2,1)} %bitcast.68), kind=kLoop, calls=%fused_computation.10 | loop fusion | flops 1310720 | bytes 1966084 | tf_op jit(solution)/shard_map/convert_element_type | solution.py:98
  89.8 4.5 %all-to-all-start.1 = ((bf16[16,20,1024]{2,1,0:T(8,128)(2,1)}), bf16[16,20,1024]{2,1,0:T(8,128)(2,1)}, u32[]{:S(2)}, u32[]{:S(2)}) async-start(bf16[16,20,1024]{2,1,0:T(8,128)(2,1)} %add_convert_fusion), calls=%async_computation.1 | async-start | bytes 1572864 | tf_op jit(solution)/shard_map/all_to_all | solution.py:100
  94.3 1.9 %compare_convert_fusion = f32[128]{0:T(128)} fusion(s32[]{:T(128)} %bitcast.16, s32[]{:T(128)} %bitcast.15), kind=kLoop, calls=%fused_computation.85 | loop fusion | flops 4352 | bytes 520 | tf_op jit(solution)/shard_map/convert_element_type | solution.py:146
  96.4 52.0 %collective-permute-done.5 = bf16[8,64,1024]{2,1,0:T(8,128)(2,1)S(1)} collective-permute-done((bf16[8,64,1024]{2,1,0:T(8,128)(2,1)S(1)}, bf16[8,64,1024]{2,1,0:T(8,128)(2,1)S(1)}, u32[]{:S(2)}, u32[]{:S(2)}) %collective-permute-start.5) | collective-permute-done | bytes 1048608 | tf_op jit(solution)/shard_map/ppermute | solution.py:20
  149.3 2.1 %convolution_convert_fusion.3 = bf16[128,1024]{1,0:T(8,128)(2,1)S(1)} fusion(bf16[1024,1024]{1,0:T(8,128)(2,1)} %all-gather.6.cloned.1.call-done, bf16[128,1024]{1,0:T(8,128)(2,1)S(1)} %copy-done, f32[1024]{0:T(1024)S(1)} %copy-done.6, f32[128]{0:T(128)S(1)} %add_rsqrt_fusion, f32[128]{0:T(128)S(1)} %broadcast_multiply_fusion.1), kind=kOutput, calls=%fused_computation.24 | convolution fusion | flops 269221888 | bytes 2626560 | tf_op jit(solution)/shard_map/dot_general | solution.py:112
  151.4 1.1 reshape.214
  152.5 3.7 %all-to-all-done.1 = bf16[16,20,1024]{2,1,0:T(8,128)(2,1)} async-done(((bf16[16,20,1024]{2,1,0:T(8,128)(2,1)}), bf16[16,20,1024]{2,1,0:T(8,128)(2,1)}, u32[]{:S(2)}, u32[]{:S(2)}) %all-to-all-start.1) | async-done | bytes 655392 | tf_op jit(solution)/shard_map/all_to_all | solution.py:100
  156.2 1.2 reshape.212
  157.4 1.2 gather_fusion
  159.6 1.3 fusion.37
  161.1 2.2 %convolution_convert_fusion.2 = bf16[128,1024]{1,0:T(8,128)(2,1)S(1)} fusion(bf16[128,1024]{1,0:T(8,128)(2,1)S(1)} %fusion.30, bf16[1024,1024]{1,0:T(8,128)(2,1)} %all-gather.8.cloned.1.call-done), kind=kOutput, calls=%fused_computation.23 | convolution fusion | flops 268566528 | bytes 2621440 | tf_op jit(solution)/shard_map/dot_general | solution.py:113
  163.3 1.1 reshape.215
  164.4 1.6 fusion.56
  166.1 2.5 %fusion.12 = f32[2,16,64,64]{2,3,1,0:T(8,128)} fusion(bf16[2,64,16,64]{3,2,1,0:T(8,128)(2,1)} %reshape.215, bf16[2,64,16,64]{3,2,1,0:T(8,128)(2,1)S(1)} %copy-done.3, pred[2,64]{1,0:T(4,128)(4,1)S(1)} %copy-done.11), kind=kOutput, calls=%fused_computation.14 | convolution fusion | flops 17039360 | bytes 1048704 | tf_op jit(solution)/shard_map/sqhd,skhd->shqk/dot_general | solution.py:121
  168.5 6.9 %all-gather.4.cloned.1.call-done = bf16[1024,1024]{1,0:T(8,128)(2,1)} async-done(((bf16[64,1024]{1,0:T(8,128)(2,1)}), bf16[1024,1024]{1,0:T(8,128)(2,1)}) %all-gather.4.cloned.1.call-update) | async-done | bytes 2097168 | tf_op jit(solution)/shard_map/all_gather | solution.py:108
  175.4 2.0 %convolution_convert_fusion.4 = bf16[128,1024]{1,0:T(8,128)(2,1)S(1)} fusion(bf16[128,1024]{1,0:T(8,128)(2,1)S(1)} %fusion.30, bf16[1024,1024]{1,0:T(8,128)(2,1)} %all-gather.4.cloned.1.call-done), kind=kOutput, calls=%fused_computation.25 | convolution fusion | flops 268566528 | bytes 2621440 | tf_op jit(solution)/shard_map/dot_general | solution.py:114
  177.8 2.9 %fusion.13 = bf16[2,64,16,64]{1,3,2,0:T(8,128)(2,1)} fusion(bf16[2,64,16,64]{3,2,1,0:T(8,128)(2,1)S(1)} %reshape.213, f32[2,16,64]{2,1,0:T(8,128)S(1)} %fusion.56, f32[2,16,64,64]{2,3,1,0:T(8,128)} %fusion.12), kind=kOutput, calls=%fused_computation.17 | convolution fusion | flops 17303616 | bytes 1056768 | tf_op jit(solution)/shard_map/shqk,skhd->sqhd/dot_general | solution.py:129
  180.7 1.5 copy.56
  182.5 1.5 fusion.17
  (81 shorter events, 14.5 us)
Async XLA Ops:
  7.2 141.6 %all-gather.6.cloned.1.call-start = ((), (), s32[]{:S(2)}) async-start(), calls=%async_computation.3 | async-start | bytes 2228224 | tf_op jit(solution)/shard_map/all_gather | solution.py:106
  7.9 153.2 %all-gather.8.cloned.1.call-start = ((), (), s32[]{:S(2)}) async-start(), calls=%async_computation.4 | async-start | bytes 2228224 | tf_op jit(solution)/shard_map/all_gather | solution.py:107
  15.4 10.5 %copy-start.4 = (bf16[64,1024]{1,0:T(8,128)(2,1)S(1)}, bf16[64,1024]{1,0:T(8,128)(2,1)}, u32[]{:S(2)}) copy-start(bf16[64,1024]{1,0:T(8,128)(2,1)} %param.27) | copy-start | bytes 393220
  18.4 32.3 %copy-start = (bf16[128,1024]{1,0:T(8,128)(2,1)S(1)}, bf16[128,1024]{1,0:T(8,128)(2,1)}, u32[]{:S(2)}) copy-start(bf16[128,1024]{1,0:T(8,128)(2,1)} %param.20) | copy-start | bytes 786436
  18.4 27.2 %all-to-all-start = ((bf16[16,20,1024]{2,1,0:T(8,128)(2,1)}), bf16[16,20,1024]{2,1,0:T(8,128)(2,1)S(1)}, u32[]{:S(2)}, u32[]{:S(2)}) async-start(bf16[16,20,1024]{2,1,0:T(8,128)(2,1)} %reshape.209), calls=%async_computation | async-start | bytes 1572864 | tf_op jit(solution)/shard_map/all_to_all | solution.py:84
  25.9 149.4 %all-gather.4.cloned.1.call-start = ((), (), s32[]{:S(2)}) async-start(), calls=%async_computation.2 | async-start | bytes 2228224 | tf_op jit(solution)/shard_map/all_gather | solution.py:108
  26.0 1.5 collective-permute-start.2
  46.0 17.7 %collective-permute-start = (bf16[16,20,1024]{2,0,1:T(8,128)(2,1)S(1)}, bf16[16,20,1024]{2,0,1:T(8,128)(2,1)S(1)}, u32[]{:S(2)}, u32[]{:S(2)}) collective-permute-start(bf16[16,20,1024]{2,0,1:T(8,128)(2,1)S(1)} %copy.48), channel_id=1, source_target_pairs={{0,1},{1,0},{2,3},{3,2},{4,5},{5,4},{6,7},{7,6},{8,9},{9,8},{10,11... | collective-permute-start | bytes 1966088 | tf_op jit(solution)/shard_map/ppermute | solution.py:37
  46.5 10.8 %collective-permute-start.3 = (bf16[2,64,1024]{2,1,0:T(8,128)(2,1)S(1)}, bf16[2,64,1024]{2,1,0:T(8,128)(2,1)S(1)}, u32[]{:S(2)}, u32[]{:S(2)}) collective-permute-start(bf16[2,64,1024]{2,1,0:T(8,128)(2,1)S(1)} %pad_maximum_fusion.4), channel_id=1, source_target_pairs={{0,2},{1,3},{2,0},{3,1},{4,6},{5,7},{6,4},{7,5},{8,10},{9,11},{10,... | collective-permute-start | bytes 786440 | tf_op jit(solution)/shard_map/ppermute | solution.py:20
  58.2 20.2 %collective-permute-start.4 = (bf16[4,64,1024]{2,1,0:T(8,128)(2,1)}, bf16[4,64,1024]{2,1,0:T(8,128)(2,1)}, u32[]{:S(2)}, u32[]{:S(2)}) collective-permute-start(bf16[4,64,1024]{2,1,0:T(8,128)(2,1)} %pad_maximum_fusion.3), channel_id=1, source_target_pairs={{0,4},{1,5},{2,6},{3,7},{4,0},{5,1},{6,2},{7,3},{8,12},{9,13},{10,... | collective-permute-start | bytes 1572872 | tf_op jit(solution)/shard_map/ppermute | solution.py:20
  74.6 12.2 %collective-permute-start.1 = (bf16[16,40,1024]{2,1,0:T(8,128)(2,1)}, bf16[16,40,1024]{2,1,0:T(8,128)(2,1)}, u32[]{:S(2)}, u32[]{:S(2)}) collective-permute-start(bf16[16,40,1024]{2,1,0:T(8,128)(2,1)} %bitcast.67), channel_id=1, source_target_pairs={{0,1},{1,0},{2,3},{3,2},{4,5},{5,4},{6,7},{7,6},{8,9},{9,8},{10,11... | collective-permute-start | bytes 3932168 | tf_op jit(solution)/shard_map/ppermute | solution.py:37
  74.8 10.8 %copy-start.7 = (s32[2]{0:T(128)S(1)}, s32[2]{0:T(128)}, u32[]{:S(2)}) copy-start(s32[2]{0:T(128)} %param.23) | copy-start | bytes 28
  74.8 11.4 %copy-start.10 = (s32[2]{0:T(128)S(1)}, s32[2]{0:T(128)}, u32[]{:S(2)}) copy-start(s32[2]{0:T(128)} %param.22) | copy-start | bytes 28
  79.6 16.8 %copy-start.8 = (f32[128,2]{0,1:T(2,128)S(1)}, f32[128,2]{0,1:T(2,128)}, u32[]{:S(2)}) copy-start(f32[128,2]{0,1:T(2,128)} %param.17) | copy-start | bytes 3076
  79.6 16.8 %copy-start.5 = (s32[128,2]{0,1:T(2,128)S(1)}, s32[128,2]{0,1:T(2,128)}, u32[]{:S(2)}) copy-start(s32[128,2]{0,1:T(2,128)} %param.16) | copy-start | bytes 3076
  79.6 68.8 %collective-permute-start.5 = (bf16[8,64,1024]{2,1,0:T(8,128)(2,1)S(1)}, bf16[8,64,1024]{2,1,0:T(8,128)(2,1)S(1)}, u32[]{:S(2)}, u32[]{:S(2)}) collective-permute-start(bf16[8,64,1024]{2,1,0:T(8,128)(2,1)S(1)} %pad_maximum_fusion.2), channel_id=1, source_target_pairs={{0,8},{1,9},{2,10},{3,11},{4,12},{5,13},{6,14},{7,15},{8,0},{9,1},... | collective-permute-start | bytes 3145736 | tf_op jit(solution)/shard_map/ppermute | solution.py:20
  89.8 66.4 %all-to-all-start.1 = ((bf16[16,20,1024]{2,1,0:T(8,128)(2,1)}), bf16[16,20,1024]{2,1,0:T(8,128)(2,1)}, u32[]{:S(2)}, u32[]{:S(2)}) async-start(bf16[16,20,1024]{2,1,0:T(8,128)(2,1)} %add_convert_fusion), calls=%async_computation.1 | async-start | bytes 1572864 | tf_op jit(solution)/shard_map/all_to_all | solution.py:100
  148.6 0.7 copy-start.6
  158.6 2.3 %copy-start.1 = (bf16[128,1024]{1,0:T(8,128)(2,1)S(1)}, bf16[128,1024]{1,0:T(8,128)(2,1)}, u32[]{:S(2)}) copy-start(bf16[128,1024]{1,0:T(8,128)(2,1)} %param.14) | copy-start | bytes 786436
  161.0 14.3 %copy-start.2 = (bf16[128,1024]{1,0:T(8,128)(2,1)}, bf16[128,1024]{1,0:T(8,128)(2,1)S(1)}, u32[]{:S(2)}) copy-start(bf16[128,1024]{1,0:T(8,128)(2,1)S(1)} %fusion.30) | copy-start | bytes 786436
  161.1 3.4 %copy-start.3 = (bf16[2,64,16,64]{3,2,1,0:T(8,128)(2,1)S(1)}, bf16[2,64,16,64]{3,2,1,0:T(8,128)(2,1)}, u32[]{:S(2)}) copy-start(bf16[2,64,16,64]{3,2,1,0:T(8,128)(2,1)} %reshape.214) | copy-start | bytes 786436
  161.1 3.3 %copy-start.11 = (pred[2,64]{1,0:T(4,128)(4,1)S(1)}, pred[2,64]{1,0:T(4,128)(4,1)}, u32[]{:S(2)}) copy-start(pred[2,64]{1,0:T(4,128)(4,1)} %iota_compare_fusion.2) | copy-start | bytes 388
  177.8 4.7 %copy-start.9 = (f32[128]{0:T(128)S(1)}, f32[128]{0:T(128)}, u32[]{:S(2)}) copy-start(f32[128]{0:T(128)} %compare_convert_fusion) | copy-start | bytes 1540
Sparse Core Ops, SparseCore 0:
  10.2 49.2 all-gather.5
  61.7 68.4 all-gather.7
  132.3 43.0 all-gather.3
